TPU v7x, 32 devices: a whole 2x2x4 slice. The times are simulated.
32 devices in a mesh: row: 4 (over x, core), col: 8 (over z, y).
Axes of the slice: x: 2, y: 2, z: 4, core: 2. Of those that a mesh axis runs over, the one named last changes fastest.
Arguments:
- features: float32 [4096, 512], P(('col', 'row')), may hold values from -6 to 6
- weight: float32 [512, 512], replicated, may hold values from -0.25 to 0.25
- cotangent: bfloat16 [4096, 512], P(('row', 'col')), may hold values from -6 to 6
- block_values: bfloat16 [4, 8, 12, 128, 128], P('row', 'col'), may hold values from -0.1875 to 0.1875
- block_coords: int32 [4, 8, 2, 12], P('row', 'col'), may hold values from -1 to 7, as said below
Outputs:
- activated: float32 [4096, 512], P(('row', 'col'))
- dfeatures: float32 [4096, 512], P(('col', 'row'))
- dweight: float32 [512, 512], P('row', 'col')
Inputs may be any that keep to these rules, and one draw needn't show every extreme that they name: block_coords[r, c, 0, s] is a block row below 8 and block_coords[r, c, 1, s] a block column below 4 of slot s of device (r, c), or both are -1 for an unused slot. Used slots come first and name distinct blocks; each device uses between a quarter of 12 (rounded down) and all 12 slots, and some device uses all 12.
All inputs are finite; a program needn't handle non-finite values.
Results may differ from a plain program's by a relative error of at most 0.006.
Values may be sent and summed in bfloat16 or wider, within the bound.
A program may use at most 128 MiB of HBM per device.

v0:
```python
import jax
import jax.numpy as jnp
from jax import lax
from jax.sharding import PartitionSpec as P


def silu_slope(values):
    sigma = jax.nn.sigmoid(values)
    return sigma * (1.0 + values * (1.0 - sigma))


def group_size(slot_count):
    return 32 if slot_count % 32 == 0 else slot_count


def blocks_forward(slot_values, slot_rows, slot_cols, tile_stack, out_blocks):
    slot_count = slot_values.shape[0]
    group = group_size(slot_count)
    turn_count = slot_count // group
    block = slot_values.shape[1]
    hidden_width = tile_stack.shape[-1]

    def add_group(totals, slot_item):
        group_vals, row_ids, col_ids = slot_item
        selected = jnp.take(tile_stack, col_ids, axis=0)
        products = jnp.einsum(
            "sab,sbc->sac", group_vals, selected, preferred_element_type=jnp.float32
        )
        return (totals.at[row_ids].add(products), None)

    zero_sums = jnp.zeros((out_blocks, block, hidden_width), jnp.float32)
    totals, _ = lax.scan(
        add_group,
        zero_sums,
        (
            slot_values.reshape(turn_count, group, block, block),
            slot_rows.reshape(turn_count, group),
            slot_cols.reshape(turn_count, group),
        ),
    )
    return totals.reshape(out_blocks * block, hidden_width)


def blocks_backward(slot_values, slot_rows, slot_cols, tile_stack, out_blocks):
    slot_count = slot_values.shape[0]
    group = group_size(slot_count)
    turn_count = slot_count // group
    block = slot_values.shape[1]
    hidden_width = tile_stack.shape[-1]

    def add_group(totals, slot_item):
        group_vals, row_ids, col_ids = slot_item
        selected = jnp.take(tile_stack, row_ids, axis=0)
        products = jnp.einsum(
            "sab,sac->sbc", group_vals, selected, preferred_element_type=jnp.float32
        )
        return (totals.at[col_ids].add(products), None)

    zero_sums = jnp.zeros((out_blocks, block, hidden_width), jnp.float32)
    totals, _ = lax.scan(
        add_group,
        zero_sums,
        (
            slot_values.reshape(turn_count, group, block, block),
            slot_rows.reshape(turn_count, group),
            slot_cols.reshape(turn_count, group),
        ),
    )
    return totals.reshape(out_blocks * block, hidden_width)


def on_device(features, weight, cotangent, block_values, block_coords):
    slot_values = block_values[0, 0]
    coordinate = block_coords[0, 0]
    live_slots = coordinate[0] >= 0
    slot_values = jnp.where(live_slots[:, None, None], slot_values, jnp.zeros_like(slot_values))
    slot_rows = jnp.maximum(coordinate[0], 0)
    slot_cols = jnp.maximum(coordinate[1], 0)
    block = slot_values.shape[1]
    own_rows = features.shape[0]
    hidden_width = features.shape[1]
    col_count = lax.axis_size("col")
    row_count = lax.axis_size("row")
    row_blocks = col_count * own_rows // block
    col_blocks = row_count * own_rows // block
    xcopy = features.astype(jnp.bfloat16)
    wcopy = weight.astype(jnp.bfloat16)
    projected = jnp.dot(xcopy, wcopy, preferred_element_type=jnp.float32).astype(jnp.bfloat16)
    column_rows = lax.all_gather(projected, "row", axis=0, tiled=True)
    partial_value = blocks_forward(
        slot_values,
        slot_rows,
        slot_cols,
        column_rows.reshape(col_blocks, block, hidden_width),
        row_blocks,
    )
    own_sums = lax.psum_scatter(partial_value, "col", scatter_dimension=0, tiled=True)
    activated = jax.nn.silu(own_sums)
    slope = (cotangent.astype(jnp.float32) * silu_slope(own_sums)).astype(jnp.bfloat16)
    slope_rows = lax.all_gather(slope, "col", axis=0, tiled=True)
    column_part = blocks_backward(
        slot_values,
        slot_rows,
        slot_cols,
        slope_rows.reshape(row_blocks, block, hidden_width),
        col_blocks,
    )
    node_grad = lax.psum_scatter(column_part, "row", scatter_dimension=0, tiled=True)
    grad_copy = node_grad.astype(jnp.bfloat16)
    dfeatures = jnp.dot(grad_copy, wcopy.T, preferred_element_type=jnp.float32)
    local_weight = jnp.dot(xcopy.T, grad_copy, preferred_element_type=jnp.float32)
    weight_part = lax.psum_scatter(local_weight, "row", scatter_dimension=0, tiled=True)
    node_total = own_rows * row_count * col_count
    dweight = lax.psum_scatter(weight_part, "col", scatter_dimension=1, tiled=True) * (
        1.0 / node_total**0.5
    )
    return (activated, dfeatures, dweight)


def solution(mesh):
    placed = (
        P(("col", "row"), None),
        P(),
        P(("row", "col"), None),
        P("row", "col", None, None, None),
        P("row", "col", None, None),
    )
    return jax.shard_map(
        on_device,
        mesh=mesh,
        in_specs=placed,
        out_specs=(P(("row", "col"), None), P(("col", "row"), None), P("row", "col")),
        check_vma=False,
    )
```

profile of v0, /device:TPU:0, one launch (start us, length us, event | category | flops | bytes accessed | tf_op | source)
XLA Modules:
  0.0 274.8 jit_solution(13468795672481042153)
XLA Ops:
  7.2 0.0 reduce-scatter.5.cloned.1.call-start
  7.2 0.8 compare_bitcast_fusion
  8.0 0.8 fusion.16
  8.7 1.5 convolution_convert_fusion
  10.3 8.6 %all_gather.6 = bf16[512,512]{1,0:T(8,128)(2,1)S(1)} all-gather(bf16[128,512]{1,0:T(8,128)(2,1)S(1)} %convolution_convert_fusion), channel_id=1, replica_groups=mesh['row'=4,'col'=8] {'row'}, dimensions={0}, use_global_device_ids=true | all-gather | bytes 655360 | tf_op jit(solution)/shard_map/all_gather | solution.py:89
  18.9 0.0 copy-start.3
  18.9 0.6 gather_fusion
  19.6 0.3 copy-done.3
  19.9 2.3 fusion.2
  22.2 0.2 broadcast_in_dim.46
  22.4 5.8 %scatter_fusion = f32[8,128,512]{2,1,0:T(8,128)S(1)} fusion(f32[8,128,512]{2,1,0:T(8,128)S(1)} %broadcast_in_dim.46, s32[12]{0:T(128)S(1)} %get-tuple-element.39, f32[12,128,512]{2,1,0:T(8,128)} %fusion.2), kind=kCustom, calls=%fused_computation.2 | custom fusion | flops 786432 | bytes 9437232 | tf_op jit(solution)/shard_map/while/body/eval_jaxpr/scatter-add | solution.py:29
  28.2 0.0 copy-start.1
  28.2 0.0 copy-start.6
  28.2 1.3 copy-done.1
  29.6 0.0 reduce-scatter.5.cloned.1.call-update
  29.6 0.0 all-gather.2.cloned.1.call-start
  29.6 68.6 %reduce-scatter.5.cloned.1.call-done = f32[128,512]{1,0:T(8,128)} async-done(((f32[1024,512]{1,0:T(8,128)}), f32[128,512]{1,0:T(8,128)}) %reduce-scatter.5.cloned.1.call-update) | async-done | bytes 262160 | tf_op jit(solution)/shard_map/reduce_scatter | solution.py:97
  98.2 0.0 copy-done.6
  98.2 1.8 multiply_convert_fusion
  100.1 0.0 all-gather.2.cloned.1.call-update
  100.1 0.0 reduce-scatter.7.cloned.1.call-start
  100.1 40.0 %all-gather.2.cloned.1.call-done = bf16[1024,512]{1,0:T(8,128)(2,1)} async-done(((bf16[128,512]{1,0:T(8,128)(2,1)}), bf16[1024,512]{1,0:T(8,128)(2,1)}) %all-gather.2.cloned.1.call-update) | async-done | bytes 1048592 | tf_op jit(solution)/shard_map/all_gather | solution.py:100
  140.2 1.9 gather_fusion.1
  142.0 2.3 fusion
  144.4 0.1 broadcast_in_dim.51
  144.5 0.0 copy-start.4
  144.5 5.7 %scatter_fusion.1 = f32[4,128,512]{2,1,0:T(8,128)S(1)} fusion(f32[4,128,512]{2,1,0:T(8,128)S(1)} %broadcast_in_dim.51, s32[12]{0:T(128)S(1)} %get-tuple-element.38, f32[12,128,512]{2,1,0:T(8,128)} %fusion), kind=kCustom, calls=%fused_computation.3 | custom fusion | flops 786432 | bytes 9437232 | tf_op jit(solution)/shard_map/while/body/eval_jaxpr/scatter-add | solution.py:57
  150.3 0.0 copy-start
  150.3 1.0 copy-done
  151.2 0.0 reduce-scatter.7.cloned.1.call-update
  151.3 0.0 copy-start.2
  151.3 0.0 reduce-scatter.9.cloned.1.call-start
  151.3 23.7 %reduce-scatter.7.cloned.1.call-done = f32[128,512]{1,0:T(8,128)} async-done(((f32[512,512]{1,0:T(8,128)}), f32[128,512]{1,0:T(8,128)}) %reduce-scatter.7.cloned.1.call-update) | async-done | bytes 262160 | tf_op jit(solution)/shard_map/reduce_scatter | solution.py:108
  175.0 0.0 copy-done.4
  175.0 0.0 copy-start.5
  175.0 2.3 convolution_bitcast_fusion
  177.3 0.0 reduce-scatter.9.cloned.1.call-update
  177.3 0.0 reduce-scatter.11.cloned.1.call-start
  177.4 25.1 %reduce-scatter.9.cloned.1.call-done = f32[128,512]{0,1:T(8,128)} async-done(((f32[512,512]{0,1:T(8,128)}), f32[128,512]{0,1:T(8,128)}) %reduce-scatter.9.cloned.1.call-update) | async-done | bytes 262160 | tf_op jit(solution)/shard_map/reduce_scatter | solution.py:112
  202.4 0.0 reduce-scatter.11.cloned.1.call-update
  202.5 0.0 copy-done.2
  202.5 0.0 copy-done.5
  202.5 1.0 fusion.9
  203.5 63.4 %reduce-scatter.11.cloned.1.call-done = f32[128,64]{0,1:T(8,128)} async-done(((f32[128,512]{0,1:T(8,128)}), f32[128,64]{0,1:T(8,128)}) %reduce-scatter.11.cloned.1.call-update) | async-done | bytes 32784 | tf_op jit(solution)/shard_map/reduce_scatter | solution.py:114
  266.9 1.4 broadcast_multiply_fusion
  (2 shorter events, 0.0 us)
Async XLA Ops:
  7.2 91.1 %reduce-scatter.5.cloned.1.call-start = ((), (), s32[]{:S(2)}) async-start(), calls=%async_computation.4 | async-start | bytes 2359296 | tf_op jit(solution)/shard_map/reduce_scatter | solution.py:97
  18.9 1.0 copy-start.3
  28.2 1.3 copy-start.1
  28.2 70.0 %copy-start.6 = (bf16[128,512]{1,0:T(8,128)(2,1)S(1)}, bf16[128,512]{1,0:T(8,128)(2,1)}, u32[]{:S(2)}) copy-start(bf16[128,512]{1,0:T(8,128)(2,1)} %param.7) | copy-start | bytes 393220
  29.6 110.6 %all-gather.2.cloned.1.call-start = ((), (), s32[]{:S(2)}) async-start(), calls=%async_computation.5 | async-start | bytes 1179648 | tf_op jit(solution)/shard_map/all_gather | solution.py:100
  100.1 74.9 %reduce-scatter.7.cloned.1.call-start = ((), (), s32[]{:S(2)}) async-start(), calls=%async_computation.6 | async-start | bytes 1310720 | tf_op jit(solution)/shard_map/reduce_scatter | solution.py:108
  144.5 30.5 %copy-start.4 = (f32[128,512]{1,0:T(8,128)S(1)}, f32[128,512]{1,0:T(8,128)}, u32[]{:S(2)}) copy-start(f32[128,512]{1,0:T(8,128)} %param.5) | copy-start | bytes 786436
  150.3 1.0 copy-start
  151.3 51.2 %copy-start.2 = (f32[512,512]{1,0:T(8,128)S(1)}, f32[512,512]{1,0:T(8,128)}, u32[]{:S(2)}) copy-start(f32[512,512]{1,0:T(8,128)} %param.6) | copy-start | bytes 3145732
  151.3 51.2 %reduce-scatter.9.cloned.1.call-start = ((), (), s32[]{:S(2)}) async-start(), calls=%async_computation.7 | async-start | bytes 1310720 | tf_op jit(solution)/shard_map/reduce_scatter | solution.py:112
  175.0 27.5 %copy-start.5 = (f32[128,512]{1,0:T(8,128)S(1)}, f32[128,512]{1,0:T(8,128)}, u32[]{:S(2)}) copy-start(f32[128,512]{1,0:T(8,128)} %reduce-scatter.7.cloned.1.call-done) | copy-start | bytes 786436
  177.3 89.5 %reduce-scatter.11.cloned.1.call-start = ((), (), s32[]{:S(2)}) async-start(), calls=%async_computation.8 | async-start | bytes 294912 | tf_op jit(solution)/shard_map/reduce_scatter | solution.py:114
Sparse Core Ops, SparseCore 0:
  29.7 68.4 reduce-scatter.4
  100.9 39.1 all-gather.1
  151.4 23.5 reduce-scatter.6
  177.5 24.8 reduce-scatter.8
  205.6 61.2 reduce-scatter.10
where the time goes:
time: 275 us
  waiting for transfers between devices  221 us (80%)
  other arithmetic  16.2 us (6%)
  between operations  13.9 us (5%)
  matrix products  9.5 us (3%)
  blocking collectives  8.62 us (3%)
  local copies, waits for them, and re-layouts  5.53 us (2%)
    reduce_scatter x1, waiting for transfers between devices, on_device(): lax.psum_scatter(partial_value, 'col', scatter_dimension=0, tiled=True)  68.6 us
    reduce_scatter x1, waiting for transfers between devices, on_device(): lax.psum_scatter(weight_part, 'col', scatter_dimension=1, tiled=True)  63.4 us
    all_gather x1, waiting for transfers between devices, on_device(): slope_rows = lax.all_gather(slope, 'col', axis=0, tiled=True)  40 us
    reduce_scatter x1, waiting for transfers between devices, on_device(): lax.psum_scatter(local_weight, 'row', scatter_dimension=0, tiled=True)  25.1 us
    reduce_scatter x1, waiting for transfers between devices, on_device(): lax.psum_scatter(column_part, 'row', scatter_dimension=0, tiled=True)  23.7 us
    all_gather x1, blocking collectives, on_device(): column_rows = lax.all_gather(projected, 'row', axis=0, tiled=True)  8.62 us
    scatter-add x1, other arithmetic, add_group(): return (totals.at[row_ids].add(products), None)  5.77 us
    scatter-add x1, other arithmetic, add_group(): return (totals.at[col_ids].add(products), None)  5.74 us
  transfers between devices with their start and end apart: 5, of which 5 were waited for; matrix products, arithmetic and copies ran while one was open for 0% of the time, Pallas kernels for 0%

commit v1 on v0

v1 whole, which is shorter than its diff:
```python
import functools

import jax
import jax.numpy as jnp
from jax import lax
from jax.experimental import pallas as pl
from jax.experimental.pallas import tpu as pltpu
from jax.sharding import PartitionSpec as P

MESH = pl.DeviceIdType.MESH
PARTS = 2
F32, BF16 = jnp.float32, jnp.bfloat16


def each(count, body):
    if count <= 8:
        for k in range(count):
            body(k)
    else:
        lax.fori_loop(0, count, lambda k, carry: (body(k), carry)[1], 0)


def inner_size(count):
    return 2 if count % 2 == 0 else 1


def dot(a, b, left=1, right=0):
    return lax.dot_general(a, b, (((left,), (right,)), ((), ())), preferred_element_type=F32)


def remote(src, dst, sent, landed, device):
    return pltpu.make_async_remote_copy(
        src_ref=src, dst_ref=dst, send_sem=sent, recv_sem=landed, device_id=device, device_id_type=MESH
    )


class Line:
    def __init__(self, name, count, device):
        self.count, self.device = count, device
        self.inner = inner_size(count)
        self.outer = count // self.inner
        self.me = lax.axis_index(name)
        self.o = self.me // self.inner
        self.i = self.me % self.inner

    def ahead(self, k):
        return lax.rem(self.o + k + 1, self.outer)

    def behind(self, k):
        return lax.rem(self.o + self.outer - k - 1, self.outer)

    def mate(self):
        return self.device(self.o * self.inner + 1 - self.i)


class Gather:
    def __init__(self, line, buf, sent, landed):
        self.line, self.buf, self.sent, self.landed = line, buf, sent, landed

    def copy(self, h, index, slot, device):
        piece = self.buf.at[h, index]
        return remote(piece, piece, self.sent.at[h, slot], self.landed.at[h, index], device)

    def start(self, h):
        line = self.line

        def far(k):
            self.copy(h, line.me, k, line.device(line.ahead(k) * line.inner + line.i)).start()

        if line.inner == 2:
            self.copy(h, line.me, line.outer - 1, line.mate()).start()
        each(line.outer - 1, far)

    def any_peer(self):
        line = self.line
        return line.device(lax.rem(line.me + 1, line.count))

    def relay(self, h, k):
        line = self.line
        index = line.behind(k) * line.inner + line.i
        self.copy(h, index, k, self.any_peer()).wait_recv()
        if line.inner == 2:
            self.copy(h, index, line.outer + k, line.mate()).start()
        return index

    def passed(self, h, k):
        line = self.line
        index = line.behind(k - 1) * line.inner + 1 - line.i
        self.copy(h, index, 0, self.any_peer()).wait_recv()
        return index

    def drain(self, h):
        line = self.line
        slots = 2 * line.outer - 1 if line.inner == 2 else line.outer - 1
        each(slots, lambda k: self.copy(h, line.me, k, self.any_peer()).wait_send())


class Scatter:
    def __init__(self, line, near, near_in, far, far_in, total, sems):
        self.line, self.total = line, total
        self.near, self.near_in, self.far, self.far_in = near, near_in, far, far_in
        self.near_sent, self.near_landed, self.far_sent, self.far_landed = sems

    def near_copy(self, h, o2):
        return remote(
            self.near.at[h, o2], self.near_in.at[h, o2], self.near_sent.at[h, o2],
            self.near_landed.at[h, o2], self.line.mate(),
        )

    def far_copy(self, h, o2, source):
        return remote(
            self.far.at[h, o2], self.far_in.at[h, source], self.far_sent.at[h, o2],
            self.far_landed.at[h, source], self.line.device(o2 * self.line.inner + self.line.i),
        )

    def start(self, h, partial):
        line = self.line

        def one(k):
            o2 = line.ahead(k)
            self.near[h, o2] = partial(h, o2 * line.inner + 1 - line.i).astype(BF16)
            self.near_copy(h, o2).start()

        if line.inner == 2:
            each(line.outer, one)

    def pair(self, h, o2, partial):
        line = self.line
        value = partial(h, o2 * line.inner + line.i)
        if line.inner == 2:
            self.near_copy(h, o2).wait_recv()
            value = value + self.near_in[h, o2].astype(F32)
        return value

    def middle(self, h, partial):
        line = self.line

        def one(k):
            o2 = line.ahead(k)
            self.far[h, o2] = self.pair(h, o2, partial).astype(BF16)
            self.far_copy(h, o2, line.o).start()

        each(line.outer - 1, one)
        self.total[h] = self.pair(h, line.o, partial)

    def end(self, h):
        line = self.line

        def one(k):
            source = line.behind(k)
            self.far_copy(h, line.ahead(0), source).wait_recv()
            self.total[h] += self.far_in[h, source].astype(F32)

        each(line.outer - 1, one)
        return self.total[h]

    def drain(self, h):
        line = self.line
        if line.inner == 2:
            each(line.outer, lambda k: self.near_copy(h, k).wait_send())
        each(line.outer - 1, lambda k: self.far_copy(h, line.ahead(k), line.o).wait_send())


def kernel(
    rows_n, cols_n, scale,
    coords, features, weight, cotangent, values,
    activated, dfeatures, dweight,
    xg, xg_sent, xg_landed,
    dense, flipped,
    c_near, c_near_in, c_far, c_far_in, c_total, c_ns, c_nl, c_fs, c_fl,
    sg, sg_sent, sg_landed,
    grad,
    e_near, e_near_in, e_far, e_far_in, e_total, e_ns, e_nl, e_fs, e_fl,
    w1, w1_in, w1_sent, w1_landed,
    w2, w2_in, w2_sent, w2_landed,
    wcopy,
):
    r, c = lax.axis_index("row"), lax.axis_index("col")
    row = Line("row", rows_n, lambda index: (index, c))
    col = Line("col", cols_n, lambda index: (r, index))
    own, hidden = features.shape
    width = hidden // PARTS
    slots, block = values.shape[0], values.shape[1]

    barrier = pltpu.get_barrier_semaphore()
    each(rows_n - 1, lambda k: pl.semaphore_signal(
        barrier, inc=1, device_id=row.device(lax.rem(r + k + 1, rows_n)), device_id_type=MESH))
    each(cols_n - 1, lambda k: pl.semaphore_signal(
        barrier, inc=1, device_id=col.device(lax.rem(c + k + 1, cols_n)), device_id_type=MESH))
    for h in range(PARTS):
        xg[h, r] = features[:, h * width:(h + 1) * width].astype(BF16)
    pl.semaphore_wait(barrier, rows_n + cols_n - 2)

    xs = Gather(row, xg, xg_sent, xg_landed)
    for h in range(PARTS):
        xs.start(h)

    wcopy[...] = weight[...].astype(BF16)
    row_blocks, col_blocks = cols_n * own // block, rows_n * own // block
    per = own // block

    def place(i):
        for j in range(col_blocks):
            def look(s, found):
                same = jnp.logical_and(coords[0, s] == i, coords[1, s] == j)
                return jnp.where(same, s, found)

            found = jnp.int32(slots)
            if slots <= 16:
                for s in range(slots):
                    found = look(s, found)
            else:
                found = lax.fori_loop(0, slots, look, found)
            piece = values[jnp.minimum(found, slots - 1)].astype(F32)
            piece = jnp.where(found < slots, piece, 0.0)
            if per == 1:
                rows, lead = pl.ds(0, block), i
            else:
                rows, lead = pl.ds((i % per) * block, block), i // per
            dense[lead, rows, j * block:(j + 1) * block] = piece.astype(BF16)
            flipped[lead, j * block:(j + 1) * block, rows] = piece.T.astype(BF16)

    each(row_blocks, place)

    agg = Scatter(col, c_near, c_near_in, c_far, c_far_in, c_total, (c_ns, c_nl, c_fs, c_fl))

    def forward(h, index):
        return dot(dense[index], xg[h].reshape(rows_n * own, width))

    for h in range(PARTS):
        each(row.outer - 1, lambda k: xs.relay(h, k))
        if row.inner == 2:
            each(row.outer, lambda k: xs.passed(h, k))
        agg.start(h, forward)
    for h in range(PARTS):
        agg.middle(h, forward)
    mixed = jnp.concatenate([agg.end(h) for h in range(PARTS)], axis=1)
    mixed16 = mixed.astype(BF16)

    slopes = Gather(col, sg, sg_sent, sg_landed)
    for h in range(PARTS):
        span = slice(h * width, (h + 1) * width)
        total = dot(mixed16, wcopy[:, span])
        sigma = jax.nn.sigmoid(total)
        slope = cotangent[:, span].astype(F32) * (sigma * (1.0 + total * (1.0 - sigma)))
        sg[h, c] = slope.astype(BF16)
        slopes.start(h)
        activated[:, span] = total * sigma

    share = hidden // rows_n
    for h in range(PARTS):
        span = slice(h * width, (h + 1) * width)
        w1[:, :, span] = dot(mixed16, sg[h, c], 0, 0).reshape(rows_n, share, width).astype(BF16)

    def w1_copy(k):
        to = lax.rem(r + k + 1, rows_n)
        return remote(w1.at[to], w1_in.at[r], w1_sent.at[to], w1_landed.at[r], row.device(to))

    each(rows_n - 1, lambda k: w1_copy(k).start())

    def backward(h, index):
        return dot(flipped[index], sg[h, index])

    def add(h, index):
        grad[h] += backward(h, index)

    for h in range(PARTS):
        grad[h] = backward(h, c)
        each(col.outer - 1, lambda k: add(h, slopes.relay(h, k)))

    nodes = Scatter(row, e_near, e_near_in, e_far, e_far_in, e_total, (e_ns, e_nl, e_fs, e_fl))

    def term(h, index):
        return grad[h, pl.ds(pl.multiple_of(index * own, own), own), :]

    def w1_wait(k):
        source = lax.rem(r + rows_n - k - 1, rows_n)
        remote(w1.at[source], w1_in.at[source], w1_sent.at[source], w1_landed.at[source],
               row.device(source)).wait_recv()
        return source

    def w2_copy(k):
        to = lax.rem(c + k + 1, cols_n)
        return remote(w2.at[to], w2_in.at[c], w2_sent.at[to], w2_landed.at[c], col.device(to))

    def w2_wait(k):
        source = lax.rem(c + cols_n - k - 1, cols_n)
        remote(w2.at[source], w2_in.at[source], w2_sent.at[source], w2_landed.at[source],
               col.device(source)).wait_recv()

    for h in range(PARTS):
        if col.inner == 2:
            each(col.outer, lambda k: add(h, slopes.passed(h, k)))
        nodes.start(h, term)
        if h == 0:
            each(rows_n - 1, w1_wait)
            w1_in[r] = w1[r]
            weight_sum = jnp.sum(w1_in[...].astype(F32), axis=0)
            w2[...] = weight_sum.T.reshape(cols_n, hidden // cols_n, share).astype(w2.dtype)
            each(cols_n - 1, lambda k: w2_copy(k).start())
            w2_in[c] = w2[c]
        nodes.middle(h, term)

    out = None
    for h in range(PARTS):
        grad16 = nodes.end(h).astype(BF16)
        piece = dot(grad16, wcopy[:, h * width:(h + 1) * width], 1, 1)
        out = piece if out is None else out + piece
    dfeatures[...] = out

    each(cols_n - 1, w2_wait)
    dweight[...] = jnp.sum(w2_in[...].astype(F32), axis=0).T * scale

    for h in range(PARTS):
        xs.drain(h)
        agg.drain(h)
        slopes.drain(h)
        nodes.drain(h)
    each(rows_n - 1, lambda k: w1_copy(k).wait_send())
    each(cols_n - 1, lambda k: w2_copy(k).wait_send())


def on_device(rows_n, cols_n, features, weight, cotangent, block_values, block_coords):
    values, coords = block_values[0, 0], block_coords[0, 0]
    own, hidden = features.shape
    width = hidden // PARTS
    row_in, col_in = inner_size(rows_n), inner_size(cols_n)
    row_out, col_out = rows_n // row_in, cols_n // col_in
    scale = 1.0 / (own * rows_n * cols_n) ** 0.5
    share_r, share_c = hidden // rows_n, hidden // cols_n
    dma = pltpu.SemaphoreType.DMA

    def gather_scratch(count, outer):
        return [
            pltpu.VMEM((PARTS, count, own, width), BF16),
            dma((PARTS, 2 * outer)),
            dma((PARTS, count)),
        ]

    def scatter_scratch(outer):
        piece = pltpu.VMEM((PARTS, outer, own, width), BF16)
        return [piece] * 4 + [pltpu.VMEM((PARTS, own, width), F32)] + [dma((PARTS, outer))] * 4

    scratch = (
        gather_scratch(rows_n, row_out)
        + [
            pltpu.VMEM((cols_n, own, rows_n * own), BF16),
            pltpu.VMEM((cols_n, rows_n * own, own), BF16),
        ]
        + scatter_scratch(col_out)
        + gather_scratch(cols_n, col_out)
        + [pltpu.VMEM((PARTS, rows_n * own, width), F32)]
        + scatter_scratch(row_out)
        + [pltpu.VMEM((rows_n, share_r, hidden), BF16)] * 2
        + [dma((rows_n,))] * 2
        + [pltpu.VMEM((cols_n, share_c, share_r), BF16)] * 2
        + [dma((cols_n,))] * 2
        + [pltpu.VMEM((hidden, hidden), BF16)]
    )
    vmem = pl.BlockSpec(memory_space=pltpu.VMEM)
    return pl.pallas_call(
        functools.partial(kernel, rows_n, cols_n, scale),
        out_shape=(
            jax.ShapeDtypeStruct((own, hidden), F32),
            jax.ShapeDtypeStruct((own, hidden), F32),
            jax.ShapeDtypeStruct((share_r, share_c), F32),
        ),
        in_specs=[pl.BlockSpec(memory_space=pltpu.SMEM)] + [vmem] * 4,
        out_specs=(vmem, vmem, vmem),
        scratch_shapes=scratch,
        compiler_params=pltpu.CompilerParams(
            collective_id=0, has_side_effects=True, vmem_limit_bytes=56 * 1024 * 1024
        ),
    )(coords, features, weight, cotangent, values)


def solution(mesh):
    placed = (
        P(("col", "row"), None),
        P(),
        P(("row", "col"), None),
        P("row", "col", None, None, None),
        P("row", "col", None, None),
    )
    return jax.shard_map(
        functools.partial(on_device, mesh.shape["row"], mesh.shape["col"]),
        mesh=mesh,
        in_specs=placed,
        out_specs=(P(("row", "col"), None), P(("col", "row"), None), P("row", "col")),
        check_vma=False,
    )
```

time: 275 us -> 57.4 us (0.21)
  waiting for transfers between devices: 221 us -> 0 us
  Pallas kernels: 0 us -> 51.7 us
  other arithmetic: 16.2 us -> 0 us
  between operations: 13.9 us -> 0.64 us
  matrix products: 9.5 us -> 0 us
  blocking collectives: 8.62 us -> 0 us
    reduce_scatter x4 -> x0, waiting for transfers between devices: 181 us -> none  [the longest x1 68.6 us: on_device(): lax.psum_scatter(partial_value, 'col', scatter_dimension=0, tiled=True)]
    pallas_call x0 -> x1, Pallas kernels: none -> 51.7 us  [on_device(): pl.pallas_call(functools.partial(kernel, rows_n, cols_n, scale), out_shap...]
    all_gather x1 -> x0, waiting for transfers between devices: 40 us -> none  [on_device(): slope_rows = lax.all_gather(slope, 'col', axis=0, tiled=True)]
    scatter-add x2 -> x0, other arithmetic: 11.5 us -> none  [the longest x1 5.77 us: add_group(): return (totals.at[row_ids].add(products), None)]
    dot_general x5 -> x0, matrix products: 9.5 us -> none  [the longest x1 2.35 us: add_group(): jnp.einsum('sab,sac->sbc', group_vals, selected, preferred_element_type=j...]
    all_gather x1 -> x0, blocking collectives: 8.62 us -> none  [on_device(): column_rows = lax.all_gather(projected, 'row', axis=0, tiled=True)]
  transfers between devices with their start and end apart: 5 -> 0, of which waited for: 5 -> 0; matrix products, arithmetic and copies ran while one was open for 0% -> 0% of each run, Pallas kernels for 0% -> 0%
where the time goes in v1:
time: 57.4 us; the launch traced here: 56.3 us
  Pallas kernels  51.7 us (90%)
  local copies, waits for them, and re-layouts  3.96 us (7%)
  between operations  0.64 us (1%)
    pallas_call x1, Pallas kernels, on_device(): pl.pallas_call(functools.partial(kernel, rows_n, cols_n, scale), out_shap...  51.7 us
    unnamed x4, local copies, waits for them, and re-layouts  2.42 us
    pallas_call x1, local copies, waits for them, and re-layouts, on_device(): pl.pallas_call(functools.partial(kernel, rows_n, cols_n, scale), out_shap...  1.54 us

profile of v1, /device:TPU:0, one launch (start us, length us, event | category | flops | bytes accessed | tf_op | source)
XLA Modules:
  0.0 56.3 jit_solution(13645641694276862212)
XLA Ops:
  0.6 51.7 %shard_map.76 = (f32[128,512]{1,0:T(8,128)}, f32[128,512]{1,0:T(8,128)}, f32[128,64]{1,0:T(8,128)}) custom-call(s32[2,12]{1,0:T(2,128)} %bitcast.3, f32[128,512]{1,0:T(8,128)} %features.1, f32[512,512]{1,0:T(8,128)} %weight.1, bf16[128,512]{1,0:T(8,128)(2,1)} %cotangent.1, bf16[12,128,128]{2,1,0:T(8,128)(2,1)} %bitcast.2), custom_call_target="tpu_custom_call" | custom-call | tf_op jit(solution)/shard_map/pallas_call | solution.py:361
  52.4 1.5 %copy.8 = f32[128,64]{0,1:T(8,128)} copy(f32[128,64]{1,0:T(8,128)} %get-tuple-element.5) | data formatting | bytes 65536 | tf_op jit(solution)/shard_map/pallas_call | solution.py:361
  53.9 0.0 copy-start
  53.9 1.7 %copy.11 = f32[128,512]{1,0:T(8,128)} copy(f32[128,512]{1,0:T(8,128)} %get-tuple-element.9) | data formatting | bytes 524288
  55.6 0.0 copy-done
  55.6 0.7 %copy.12 = f32[128,512]{1,0:T(8,128)} copy(f32[128,512]{1,0:T(8,128)S(1)} %copy-done) | data formatting | bytes 524288
Async XLA Ops:
  53.9 1.7 %copy-start = (f32[128,512]{1,0:T(8,128)S(1)}, f32[128,512]{1,0:T(8,128)}, u32[]{:S(2)}) copy-start(f32[128,512]{1,0:T(8,128)} %get-tuple-element.10) | copy-start | bytes 786436

commit v2 on v1

--- a/solution.py
+++ b/solution.py
@@ -173,7 +173,7 @@
     e_near, e_near_in, e_far, e_far_in, e_total, e_ns, e_nl, e_fs, e_fl,
     w1, w1_in, w1_sent, w1_landed,
     w2, w2_in, w2_sent, w2_landed,
-    wcopy,
+    wcopy, wide, mixed, stock, fetched,
 ):
     r, c = lax.axis_index("row"), lax.axis_index("col")
     row = Line("row", rows_n, lambda index: (index, c))
@@ -187,40 +187,51 @@
         barrier, inc=1, device_id=row.device(lax.rem(r + k + 1, rows_n)), device_id_type=MESH))
     each(cols_n - 1, lambda k: pl.semaphore_signal(
         barrier, inc=1, device_id=col.device(lax.rem(c + k + 1, cols_n)), device_id_type=MESH))
+    fetch_values = pltpu.make_async_copy(values, stock.at[pl.ds(0, slots)], fetched.at[0])
+    fetch_weight = pltpu.make_async_copy(weight, wide, fetched.at[1])
+    fetch_values.start()
+    fetch_weight.start()
     for h in range(PARTS):
         xg[h, r] = features[:, h * width:(h + 1) * width].astype(BF16)
+    stock[slots] = jnp.zeros((block, block), BF16)
     pl.semaphore_wait(barrier, rows_n + cols_n - 2)
 
     xs = Gather(row, xg, xg_sent, xg_landed)
     for h in range(PARTS):
         xs.start(h)
 
-    wcopy[...] = weight[...].astype(BF16)
     row_blocks, col_blocks = cols_n * own // block, rows_n * own // block
     per = own // block
+    short = slots <= 16
+    keys = [coords[0, s] * col_blocks + coords[1, s] for s in range(slots)] if short else None
 
     def place(i):
         for j in range(col_blocks):
             def look(s, found):
-                same = jnp.logical_and(coords[0, s] == i, coords[1, s] == j)
-                return jnp.where(same, s, found)
+                key = keys[s] if short else coords[0, s] * col_blocks + coords[1, s]
+                return jnp.where(key == i * col_blocks + j, s, found)
 
             found = jnp.int32(slots)
-            if slots <= 16:
+            if short:
                 for s in range(slots):
                     found = look(s, found)
             else:
                 found = lax.fori_loop(0, slots, look, found)
-            piece = values[jnp.minimum(found, slots - 1)].astype(F32)
-            piece = jnp.where(found < slots, piece, 0.0)
+            piece = stock[found]
             if per == 1:
                 rows, lead = pl.ds(0, block), i
             else:
                 rows, lead = pl.ds((i % per) * block, block), i // per
-            dense[lead, rows, j * block:(j + 1) * block] = piece.astype(BF16)
-            flipped[lead, j * block:(j + 1) * block, rows] = piece.T.astype(BF16)
-
-    each(row_blocks, place)
+            dense[lead, rows, j * block:(j + 1) * block] = piece
+            flipped[lead, j * block:(j + 1) * block, rows] = piece.T
+
+    fetch_values.wait()
+    half = row_blocks // 2
+    each(half, place)
+    each(row.outer - 1, lambda k: xs.relay(0, k))
+    each(row_blocks - half, lambda k: place(half + k))
+    for h in range(1, PARTS):
+        each(row.outer - 1, lambda k: xs.relay(h, k))
 
     agg = Scatter(col, c_near, c_near_in, c_far, c_far_in, c_total, (c_ns, c_nl, c_fs, c_fl))
 
@@ -228,19 +239,25 @@
         return dot(dense[index], xg[h].reshape(rows_n * own, width))
 
     for h in range(PARTS):
-        each(row.outer - 1, lambda k: xs.relay(h, k))
         if row.inner == 2:
             each(row.outer, lambda k: xs.passed(h, k))
         agg.start(h, forward)
+    fetch_weight.wait()
+    wcopy[...] = wide[...].astype(BF16)
     for h in range(PARTS):
         agg.middle(h, forward)
-    mixed = jnp.concatenate([agg.end(h) for h in range(PARTS)], axis=1)
-    mixed16 = mixed.astype(BF16)
+    for h in range(PARTS):
+        span = slice(h * width, (h + 1) * width)
+        part = agg.end(h).astype(BF16)
+        mixed[:, span] = part
+        term = dot(part, wcopy[span, :])
+        activated[...] = term if h == 0 else activated[...] + term
+    mixed16 = mixed[...]
 
     slopes = Gather(col, sg, sg_sent, sg_landed)
     for h in range(PARTS):
         span = slice(h * width, (h + 1) * width)
-        total = dot(mixed16, wcopy[:, span])
+        total = activated[:, span]
         sigma = jax.nn.sigmoid(total)
         slope = cotangent[:, span].astype(F32) * (sigma * (1.0 + total * (1.0 - sigma)))
         sg[h, c] = slope.astype(BF16)
@@ -309,7 +326,7 @@
     dfeatures[...] = out
 
     each(cols_n - 1, w2_wait)
-    dweight[...] = jnp.sum(w2_in[...].astype(F32), axis=0).T * scale
+    dweight[...] = jnp.sum(w2_in[...].astype(F32), axis=0) * scale
 
     for h in range(PARTS):
         xs.drain(h)
@@ -318,6 +335,17 @@
         nodes.drain(h)
     each(rows_n - 1, lambda k: w1_copy(k).wait_send())
     each(cols_n - 1, lambda k: w2_copy(k).wait_send())
+
+
+def hand_over(a, b, c, a_out, b_out, c_out, sems):
+    copies = [
+        pltpu.make_async_copy(src, dst, sems.at[k])
+        for k, (src, dst) in enumerate(((a, a_out), (b, b_out), (c, c_out)))
+    ]
+    for copy in copies:
+        copy.start()
+    for copy in copies:
+        copy.wait()
 
 
 def on_device(rows_n, cols_n, features, weight, cotangent, block_values, block_coords):
@@ -355,23 +383,39 @@
         + [dma((rows_n,))] * 2
         + [pltpu.VMEM((cols_n, share_c, share_r), BF16)] * 2
         + [dma((cols_n,))] * 2
-        + [pltpu.VMEM((hidden, hidden), BF16)]
+        + [
+            pltpu.VMEM((hidden, hidden), BF16),
+            pltpu.VMEM((hidden, hidden), F32),
+            pltpu.VMEM((own, hidden), BF16),
+            pltpu.VMEM((values.shape[0] + 1,) + values.shape[1:], BF16),
+            dma((2,)),
+        ]
     )
     vmem = pl.BlockSpec(memory_space=pltpu.VMEM)
-    return pl.pallas_call(
+    anywhere = pl.BlockSpec(memory_space=pl.ANY)
+    results = pl.pallas_call(
         functools.partial(kernel, rows_n, cols_n, scale),
         out_shape=(
             jax.ShapeDtypeStruct((own, hidden), F32),
             jax.ShapeDtypeStruct((own, hidden), F32),
-            jax.ShapeDtypeStruct((share_r, share_c), F32),
+            jax.ShapeDtypeStruct((share_c, share_r), F32),
         ),
-        in_specs=[pl.BlockSpec(memory_space=pltpu.SMEM)] + [vmem] * 4,
+        in_specs=[pl.BlockSpec(memory_space=pltpu.SMEM), vmem, anywhere, vmem, anywhere],
         out_specs=(vmem, vmem, vmem),
         scratch_shapes=scratch,
         compiler_params=pltpu.CompilerParams(
             collective_id=0, has_side_effects=True, vmem_limit_bytes=56 * 1024 * 1024
         ),
     )(coords, features, weight, cotangent, values)
+    ours, theirs, turned = pl.pallas_call(
+        hand_over,
+        out_shape=tuple(jax.ShapeDtypeStruct(a.shape, a.dtype) for a in results),
+        in_specs=[pl.BlockSpec(memory_space=pltpu.HBM)] * 3,
+        out_specs=(pl.BlockSpec(memory_space=pltpu.HBM),) * 3,
+        scratch_shapes=[dma((3,))],
+        compiler_params=pltpu.CompilerParams(vmem_limit_bytes=60 * 1024 * 1024),
+    )(*results)
+    return ours, theirs, turned.T
 
 
 def solution(mesh):

time: 57.4 us -> 71.6 us (1.25)
  the two profiles are of different devices: /device:TPU:0 before, /device:TPU:25 now
where the time goes in v2:
time: 71.6 us; the launch traced here: 71.5 us
  Pallas kernels  70.8 us (99%)
    pallas_call x1, Pallas kernels, on_device(): pl.pallas_call(functools.partial(kernel, rows_n, cols_n, scale), out_shap...  52.8 us
    pallas_call x1, Pallas kernels, on_device(): pl.pallas_call(hand_over, out_shape=tuple((jax.ShapeDtypeStruct(a.shape,...  18 us

profile of v2, /device:TPU:25, one launch (start us, length us, event | category | flops | bytes accessed | tf_op | source)
XLA Modules:
  0.0 71.5 jit_solution(724256772911086944)
XLA Ops:
  0.6 52.8 %shard_map.76 = (f32[128,512]{1,0:T(8,128)}, f32[128,512]{1,0:T(8,128)}, f32[64,128]{1,0:T(8,128)}) custom-call(s32[2,12]{1,0:T(2,128)} %bitcast.4, f32[128,512]{1,0:T(8,128)} %features.1, f32[512,512]{1,0:T(8,128)} %weight.1, bf16[128,512]{1,0:T(8,128)(2,1)} %cotangent.1, bf16[12,128,128]{2,1,0:T(8,128)(2,1)} %bitcast.3), custom_call_target="tpu_custom_call" | custom-call | tf_op jit(solution)/shard_map/pallas_call | solution.py:396
  53.5 18.0 %shard_map.77 = (f32[128,512]{1,0:T(8,128)}, f32[128,512]{1,0:T(8,128)}, f32[64,128]{1,0:T(8,128)}) custom-call(f32[128,512]{1,0:T(8,128)} %get-tuple-element.9.a, f32[128,512]{1,0:T(8,128)} %get-tuple-element.10.b, f32[64,128]{1,0:T(8,128)} %get-tuple-element.11.c), custom_call_target="tpu_custom_call" | custom-call | tf_op jit(solution)/shard_map/pallas_call | solution.py:410

commit v3 on v2

--- a/solution.py
+++ b/solution.py
@@ -93,6 +93,89 @@
         line = self.line
         slots = 2 * line.outer - 1 if line.inner == 2 else line.outer - 1
         each(slots, lambda k: self.copy(h, line.me, k, self.any_peer()).wait_send())
+
+
+class Chain:
+    def __init__(self, line, buf, sent, landed):
+        self.line, self.buf, self.sent, self.landed = line, buf, sent, landed
+
+    def copy(self, h, index, way, device):
+        piece = self.buf.at[h, index]
+        return remote(
+            piece, piece, self.sent.at[h, index // self.line.inner, way], self.landed.at[h, index], device
+        )
+
+    def side(self, way):
+        line = self.line
+        step = 1 if way == 0 else -1
+        there = line.o + step
+        inside = there < line.outer if way == 0 else there >= 0
+        device = line.device(lax.rem(there + line.outer, line.outer) * line.inner + line.i)
+        return inside, device
+
+    def spread(self, h, index, ways):
+        for way in ways:
+            inside, device = self.side(way)
+
+            @pl.when(inside)
+            def _():
+                self.copy(h, index, way, device).start()
+
+        if self.line.inner == 2:
+            self.copy(h, index, 2, self.line.mate()).start()
+
+    def start(self, h):
+        self.spread(h, self.line.me, (0, 1))
+
+    def other(self):
+        line = self.line
+        return line.device(lax.rem(line.me + 1, line.count))
+
+    def each_source(self, k, body):
+        line = self.line
+        for way, source in ((0, line.o - 1 - k), (1, line.o + 1 + k)):
+            pl.when(jnp.logical_and(source >= 0, source < line.outer))(
+                functools.partial(body, way, source))
+
+    def relay(self, k, hidden_parts, use):
+        def arrived(way, source):
+            index = source * self.line.inner + self.line.i
+            for h in hidden_parts:
+                self.copy(h, index, way, self.other()).wait_recv()
+                self.spread(h, index, (way,))
+            for h in hidden_parts:
+                use(h, index)
+
+        self.each_source(k, arrived)
+
+    def passed(self, k, h, use):
+        def arrived(way, source):
+            index = source * self.line.inner + 1 - self.line.i
+            self.copy(h, index, 2, self.other()).wait_recv()
+            use(h, index)
+
+        if isinstance(k, int) and k < 0:
+            arrived(2, self.line.o)
+        else:
+            self.each_source(k, arrived)
+
+    def drain(self, h):
+        line = self.line
+
+        def one(source):
+            index = source * line.inner + line.i
+            for way in (0, 1):
+                inside, device = self.side(way)
+                went = source <= line.o if way == 0 else source >= line.o
+
+                @pl.when(jnp.logical_and(inside, went))
+                def _():
+                    self.copy(h, index, way, device).wait_send()
+
+            if line.inner == 2:
+                self.copy(h, index, 2, line.mate()).wait_send()
+
+        each(line.outer, one)
 
 
 class Scatter:
@@ -254,7 +337,7 @@
         activated[...] = term if h == 0 else activated[...] + term
     mixed16 = mixed[...]
 
-    slopes = Gather(col, sg, sg_sent, sg_landed)
+    slopes = Chain(col, sg, sg_sent, sg_landed)
     for h in range(PARTS):
         span = slice(h * width, (h + 1) * width)
         total = activated[:, span]
@@ -283,7 +366,7 @@
 
     for h in range(PARTS):
         grad[h] = backward(h, c)
-        each(col.outer - 1, lambda k: add(h, slopes.relay(h, k)))
+    each(col.outer - 1, lambda k: slopes.relay(k, range(PARTS), add))
 
     nodes = Scatter(row, e_near, e_near_in, e_far, e_far_in, e_total, (e_ns, e_nl, e_fs, e_fl))
 
@@ -307,7 +390,8 @@
 
     for h in range(PARTS):
         if col.inner == 2:
-            each(col.outer, lambda k: add(h, slopes.passed(h, k)))
+            slopes.passed(-1, h, add)
+            each(col.outer - 1, lambda k: slopes.passed(k, h, add))
         nodes.start(h, term)
         if h == 0:
             each(rows_n - 1, w1_wait)
@@ -337,14 +421,16 @@
     each(cols_n - 1, lambda k: w2_copy(k).wait_send())
 
 
-def hand_over(a, b, c, a_out, b_out, c_out, sems):
-    copies = [
-        pltpu.make_async_copy(src, dst, sems.at[k])
-        for k, (src, dst) in enumerate(((a, a_out), (b, b_out), (c, c_out)))
-    ]
-    for copy in copies:
+def hand_over(a, b, c, a_out, b_out, c_out, a_held, b_held, c_held, sems):
+    rows = ((a, a_held, a_out), (b, b_held, b_out), (c, c_held, c_out))
+    ins = [pltpu.make_async_copy(src, held, sems.at[0, k]) for k, (src, held, _) in enumerate(rows)]
+    outs = [pltpu.make_async_copy(held, dst, sems.at[1, k]) for k, (_, held, dst) in enumerate(rows)]
+    for copy in ins:
         copy.start()
-    for copy in copies:
+    for copy, after in zip(ins, outs):
+        copy.wait()
+        after.start()
+    for copy in outs:
         copy.wait()
 
 
@@ -376,7 +462,11 @@
             pltpu.VMEM((cols_n, rows_n * own, own), BF16),
         ]
         + scatter_scratch(col_out)
-        + gather_scratch(cols_n, col_out)
+        + [
+            pltpu.VMEM((PARTS, cols_n, own, width), BF16),
+            dma((PARTS, col_out, 3)),
+            dma((PARTS, cols_n)),
+        ]
         + [pltpu.VMEM((PARTS, rows_n * own, width), F32)]
         + scatter_scratch(row_out)
         + [pltpu.VMEM((rows_n, share_r, hidden), BF16)] * 2
@@ -412,7 +502,7 @@
         out_shape=tuple(jax.ShapeDtypeStruct(a.shape, a.dtype) for a in results),
         in_specs=[pl.BlockSpec(memory_space=pltpu.HBM)] * 3,
         out_specs=(pl.BlockSpec(memory_space=pltpu.HBM),) * 3,
-        scratch_shapes=[dma((3,))],
+        scratch_shapes=[pltpu.VMEM(a.shape, a.dtype) for a in results] + [dma((2, 3))],
         compiler_params=pltpu.CompilerParams(vmem_limit_bytes=60 * 1024 * 1024),
     )(*results)
     return ours, theirs, turned.T

time: 71.6 us -> 55.7 us (0.78)
  the two profiles are of different devices: /device:TPU:25 before, /device:TPU:0 now
where the time goes in v3:
time: 55.7 us; the launch traced here: 55.5 us
  Pallas kernels  54.9 us (99%)
  between operations  0.64 us (1%)
    pallas_call x1, Pallas kernels, on_device(): pl.pallas_call(functools.partial(kernel, rows_n, cols_n, scale), out_shap...  53.1 us
    pallas_call x1, Pallas kernels, on_device(): pl.pallas_call(hand_over, out_shape=tuple((jax.ShapeDtypeStruct(a.shape,...  1.79 us

profile of v3, /device:TPU:0, one launch (start us, length us, event | category | flops | bytes accessed | tf_op | source)
XLA Modules:
  0.0 55.5 jit_solution(1391412153684413414)
XLA Ops:
  0.6 53.1 %shard_map.76 = (f32[128,512]{1,0:T(8,128)}, f32[128,512]{1,0:T(8,128)}, f32[64,128]{1,0:T(8,128)}) custom-call(s32[2,12]{1,0:T(2,128)} %bitcast.4, f32[128,512]{1,0:T(8,128)} %features.1, f32[512,512]{1,0:T(8,128)} %weight.1, bf16[128,512]{1,0:T(8,128)(2,1)} %cotangent.1, bf16[12,128,128]{2,1,0:T(8,128)(2,1)} %bitcast.3), custom_call_target="tpu_custom_call" | custom-call | tf_op jit(solution)/shard_map/pallas_call | solution.py:486
  53.7 1.8 %shard_map.77 = (f32[128,512]{1,0:T(8,128)}, f32[128,512]{1,0:T(8,128)}, f32[64,128]{1,0:T(8,128)}) custom-call(f32[128,512]{1,0:T(8,128)} %get-tuple-element.9.a, f32[128,512]{1,0:T(8,128)} %get-tuple-element.10.b, f32[64,128]{1,0:T(8,128)} %get-tuple-element.11.c), custom_call_target="tpu_custom_call" | custom-call | tf_op jit(solution)/shard_map/pallas_call | solution.py:500

commit v4 on v3

--- a/solution.py
+++ b/solution.py
@@ -8,7 +8,7 @@
 from jax.sharding import PartitionSpec as P
 
 MESH = pl.DeviceIdType.MESH
-PARTS = 2
+PARTS = 4
 F32, BF16 = jnp.float32, jnp.bfloat16
 
 

time: 55.7 us -> 57 us (1.023)
  Pallas kernels: 54.9 us -> 56.2 us
    pallas_call x1, Pallas kernels: 53.1 us -> 54.4 us  [on_device(): pl.pallas_call(functools.partial(kernel, rows_n, cols_n, scale), out_shap...]
where the time goes in v4:
time: 57 us; the launch traced here: 56.8 us
  Pallas kernels  56.2 us (99%)
  between operations  0.64 us (1%)
    pallas_call x1, Pallas kernels, on_device(): pl.pallas_call(functools.partial(kernel, rows_n, cols_n, scale), out_shap...  54.4 us
    pallas_call x1, Pallas kernels, on_device(): pl.pallas_call(hand_over, out_shape=tuple((jax.ShapeDtypeStruct(a.shape,...  1.79 us

profile of v4, /device:TPU:0, one launch (start us, length us, event | category | flops | bytes accessed | tf_op | source)
XLA Modules:
  0.0 56.8 jit_solution(2794982367869173472)
XLA Ops:
  0.6 54.4 %shard_map.76 = (f32[128,512]{1,0:T(8,128)}, f32[128,512]{1,0:T(8,128)}, f32[64,128]{1,0:T(8,128)}) custom-call(s32[2,12]{1,0:T(2,128)} %bitcast.4, f32[128,512]{1,0:T(8,128)} %features.1, f32[512,512]{1,0:T(8,128)} %weight.1, bf16[128,512]{1,0:T(8,128)(2,1)} %cotangent.1, bf16[12,128,128]{2,1,0:T(8,128)(2,1)} %bitcast.3), custom_call_target="tpu_custom_call" | custom-call | tf_op jit(solution)/shard_map/pallas_call | solution.py:486
  55.0 1.8 %shard_map.77 = (f32[128,512]{1,0:T(8,128)}, f32[128,512]{1,0:T(8,128)}, f32[64,128]{1,0:T(8,128)}) custom-call(f32[128,512]{1,0:T(8,128)} %get-tuple-element.9.a, f32[128,512]{1,0:T(8,128)} %get-tuple-element.10.b, f32[64,128]{1,0:T(8,128)} %get-tuple-element.11.c), custom_call_target="tpu_custom_call" | custom-call | tf_op jit(solution)/shard_map/pallas_call | solution.py:500

commit v5 on v3

--- a/solution.py
+++ b/solution.py
@@ -137,14 +137,13 @@
             pl.when(jnp.logical_and(source >= 0, source < line.outer))(
                 functools.partial(body, way, source))
 
-    def relay(self, k, hidden_parts, use):
+    def relay(self, k, h, use):
         def arrived(way, source):
             index = source * self.line.inner + self.line.i
-            for h in hidden_parts:
-                self.copy(h, index, way, self.other()).wait_recv()
-                self.spread(h, index, (way,))
-            for h in hidden_parts:
-                use(h, index)
+            self.copy(h, index, way, self.other()).wait_recv()
+            self.spread(h, index, (way,))
+            if use is not None:
+                use(index)
 
         self.each_source(k, arrived)
 
@@ -152,7 +151,8 @@
         def arrived(way, source):
             index = source * self.line.inner + 1 - self.line.i
             self.copy(h, index, 2, self.other()).wait_recv()
-            use(h, index)
+            if use is not None:
+                use(index)
 
         if isinstance(k, int) and k < 0:
             arrived(2, self.line.o)
@@ -215,16 +215,17 @@
             value = value + self.near_in[h, o2].astype(F32)
         return value
 
-    def middle(self, h, partial):
+    def middle(self, h, partial, first, last):
         line = self.line
 
         def one(k):
-            o2 = line.ahead(k)
+            o2 = line.ahead(first + k)
             self.far[h, o2] = self.pair(h, o2, partial).astype(BF16)
             self.far_copy(h, o2, line.o).start()
 
-        each(line.outer - 1, one)
-        self.total[h] = self.pair(h, line.o, partial)
+        each(last - first, one)
+        if last == line.outer - 1:
+            self.total[h] = self.pair(h, line.o, partial)
 
     def end(self, h):
         line = self.line
@@ -318,39 +319,49 @@
 
     agg = Scatter(col, c_near, c_near_in, c_far, c_far_in, c_total, (c_ns, c_nl, c_fs, c_fl))
 
-    def forward(h, index):
-        return dot(dense[index], xg[h].reshape(rows_n * own, width))
+    tall = own // PARTS
+
+    def forward(p, index):
+        rows = dense[index, p * tall:(p + 1) * tall, :]
+        return jnp.concatenate(
+            [dot(rows, xg[h].reshape(rows_n * own, width)) for h in range(PARTS)], axis=1)
 
     for h in range(PARTS):
         if row.inner == 2:
             each(row.outer, lambda k: xs.passed(h, k))
-        agg.start(h, forward)
+    for p in range(PARTS):
+        agg.start(p, forward)
     fetch_weight.wait()
     wcopy[...] = wide[...].astype(BF16)
-    for h in range(PARTS):
-        agg.middle(h, forward)
-    for h in range(PARTS):
-        span = slice(h * width, (h + 1) * width)
-        part = agg.end(h).astype(BF16)
-        mixed[:, span] = part
-        term = dot(part, wcopy[span, :])
-        activated[...] = term if h == 0 else activated[...] + term
-    mixed16 = mixed[...]
 
     slopes = Chain(col, sg, sg_sent, sg_landed)
-    for h in range(PARTS):
-        span = slice(h * width, (h + 1) * width)
-        total = activated[:, span]
+
+    def own_slope(p):
+        span = slice(p * tall, (p + 1) * tall)
+        part = agg.end(p).astype(BF16)
+        total = dot(part, wcopy[...])
         sigma = jax.nn.sigmoid(total)
-        slope = cotangent[:, span].astype(F32) * (sigma * (1.0 + total * (1.0 - sigma)))
-        sg[h, c] = slope.astype(BF16)
-        slopes.start(h)
-        activated[:, span] = total * sigma
+        slope = cotangent[span, :].astype(F32) * (sigma * (1.0 + total * (1.0 - sigma)))
+        sg[p, c] = slope.astype(BF16)
+        slopes.start(p)
+        mixed[span, :] = part
+        activated[span, :] = total * sigma
+
+    hops = col.outer - 1
+    for p in range(PARTS):
+        early = (hops + 1) // 2 if p else hops
+        agg.middle(p, forward, 0, early)
+        if p:
+            own_slope(p - 1)
+            agg.middle(p, forward, early, hops)
+            each(min(hops, 1), lambda k: slopes.relay(k, p - 1, None))
+    own_slope(PARTS - 1)
+
+    def both(index):
+        return jnp.concatenate([sg[p, index] for p in range(PARTS)], axis=0)
 
     share = hidden // rows_n
-    for h in range(PARTS):
-        span = slice(h * width, (h + 1) * width)
-        w1[:, :, span] = dot(mixed16, sg[h, c], 0, 0).reshape(rows_n, share, width).astype(BF16)
+    w1[...] = dot(mixed[...], both(c), 0, 0).reshape(rows_n, share, hidden).astype(BF16)
 
     def w1_copy(k):
         to = lax.rem(r + k + 1, rows_n)
@@ -359,14 +370,18 @@
     each(rows_n - 1, lambda k: w1_copy(k).start())
 
     def backward(h, index):
-        return dot(flipped[index], sg[h, index])
-
-    def add(h, index):
-        grad[h] += backward(h, index)
-
-    for h in range(PARTS):
-        grad[h] = backward(h, c)
-    each(col.outer - 1, lambda k: slopes.relay(k, range(PARTS), add))
+        return dot(flipped[index], both(index)[:, h * width:(h + 1) * width])
+
+    def add(index):
+        for h in range(PARTS):
+            grad[h] += backward(h, index)
+
+    for p in range(PARTS):
+        seen = min(hops, 1) if p < PARTS - 1 else 0
+        each(hops - seen, lambda k: slopes.relay(seen + k, p, add if p == PARTS - 1 else None))
+        if p == 0:
+            for h in range(PARTS):
+                grad[h] = backward(h, c)
 
     nodes = Scatter(row, e_near, e_near_in, e_far, e_far_in, e_total, (e_ns, e_nl, e_fs, e_fl))
 
@@ -388,19 +403,22 @@
         remote(w2.at[source], w2_in.at[source], w2_sent.at[source], w2_landed.at[source],
                col.device(source)).wait_recv()
 
-    for h in range(PARTS):
+    each(rows_n - 1, w1_wait)
+    w1_in[r] = w1[r]
+    weight_sum = jnp.sum(w1_in[...].astype(F32), axis=0)
+    w2[...] = weight_sum.T.reshape(cols_n, hidden // cols_n, share).astype(w2.dtype)
+    each(cols_n - 1, lambda k: w2_copy(k).start())
+    w2_in[c] = w2[c]
+
+    for p in range(PARTS):
         if col.inner == 2:
-            slopes.passed(-1, h, add)
-            each(col.outer - 1, lambda k: slopes.passed(k, h, add))
+            use = add if p == PARTS - 1 else None
+            slopes.passed(-1, p, use)
+            each(hops, lambda k: slopes.passed(k, p, use))
+    for h in range(PARTS):
         nodes.start(h, term)
-        if h == 0:
-            each(rows_n - 1, w1_wait)
-            w1_in[r] = w1[r]
-            weight_sum = jnp.sum(w1_in[...].astype(F32), axis=0)
-            w2[...] = weight_sum.T.reshape(cols_n, hidden // cols_n, share).astype(w2.dtype)
-            each(cols_n - 1, lambda k: w2_copy(k).start())
-            w2_in[c] = w2[c]
-        nodes.middle(h, term)
+    for h in range(PARTS):
+        nodes.middle(h, term, 0, row.outer - 1)
 
     out = None
     for h in range(PARTS):
@@ -451,9 +469,12 @@
             dma((PARTS, count)),
         ]
 
-    def scatter_scratch(outer):
-        piece = pltpu.VMEM((PARTS, outer, own, width), BF16)
-        return [piece] * 4 + [pltpu.VMEM((PARTS, own, width), F32)] + [dma((PARTS, outer))] * 4
+    def scatter_scratch(outer, piece):
+        return (
+            [pltpu.VMEM((PARTS, outer) + piece, BF16)] * 4
+            + [pltpu.VMEM((PARTS,) + piece, F32)]
+            + [dma((PARTS, outer))] * 4
+        )
 
     scratch = (
         gather_scratch(rows_n, row_out)
@@ -461,14 +482,14 @@
             pltpu.VMEM((cols_n, own, rows_n * own), BF16),
             pltpu.VMEM((cols_n, rows_n * own, own), BF16),
         ]
-        + scatter_scratch(col_out)
+        + scatter_scratch(col_out, (own // PARTS, hidden))
         + [
-            pltpu.VMEM((PARTS, cols_n, own, width), BF16),
+            pltpu.VMEM((PARTS, cols_n, own // PARTS, hidden), BF16),
             dma((PARTS, col_out, 3)),
             dma((PARTS, cols_n)),
         ]
         + [pltpu.VMEM((PARTS, rows_n * own, width), F32)]
-        + scatter_scratch(row_out)
+        + scatter_scratch(row_out, (own, width))
         + [pltpu.VMEM((rows_n, share_r, hidden), BF16)] * 2
         + [dma((rows_n,))] * 2
         + [pltpu.VMEM((cols_n, share_c, share_r), BF16)] * 2

time: 55.7 us -> 55.4 us (level)
  no operation moved by 1% of the time
where the time goes in v5:
time: 55.4 us; the launch traced here: 55.3 us
  Pallas kernels  54.6 us (99%)
  between operations  0.64 us (1%)
    pallas_call x1, Pallas kernels, on_device(): pl.pallas_call(functools.partial(kernel, rows_n, cols_n, scale), out_shap...  52.8 us
    pallas_call x1, Pallas kernels, on_device(): pl.pallas_call(hand_over, out_shape=tuple((jax.ShapeDtypeStruct(a.shape,...  1.79 us

profile of v5, /device:TPU:0, one launch (start us, length us, event | category | flops | bytes accessed | tf_op | source)
XLA Modules:
  0.0 55.3 jit_solution(5782523244737814049)
XLA Ops:
  0.6 52.8 %shard_map.76 = (f32[128,512]{1,0:T(8,128)}, f32[128,512]{1,0:T(8,128)}, f32[64,128]{1,0:T(8,128)}) custom-call(s32[2,12]{1,0:T(2,128)} %bitcast.4, f32[128,512]{1,0:T(8,128)} %features.1, f32[512,512]{1,0:T(8,128)} %weight.1, bf16[128,512]{1,0:T(8,128)(2,1)} %cotangent.1, bf16[12,128,128]{2,1,0:T(8,128)(2,1)} %bitcast.3), custom_call_target="tpu_custom_call" | custom-call | tf_op jit(solution)/shard_map/pallas_call | solution.py:507
  53.5 1.8 %shard_map.77 = (f32[128,512]{1,0:T(8,128)}, f32[128,512]{1,0:T(8,128)}, f32[64,128]{1,0:T(8,128)}) custom-call(f32[128,512]{1,0:T(8,128)} %get-tuple-element.9.a, f32[128,512]{1,0:T(8,128)} %get-tuple-element.10.b, f32[64,128]{1,0:T(8,128)} %get-tuple-element.11.c), custom_call_target="tpu_custom_call" | custom-call | tf_op jit(solution)/shard_map/pallas_call | solution.py:521

commit v6 on v5

--- a/solution.py
+++ b/solution.py
@@ -201,7 +201,8 @@
 
         def one(k):
             o2 = line.ahead(k)
-            self.near[h, o2] = partial(h, o2 * line.inner + 1 - line.i).astype(BF16)
+            if partial is not None:
+                self.near[h, o2] = partial(h, o2 * line.inner + 1 - line.i).astype(BF16)
             self.near_copy(h, o2).start()
 
         if line.inner == 2:
@@ -257,7 +258,7 @@
     e_near, e_near_in, e_far, e_far_in, e_total, e_ns, e_nl, e_fs, e_fl,
     w1, w1_in, w1_sent, w1_landed,
     w2, w2_in, w2_sent, w2_landed,
-    wcopy, wide, mixed, stock, fetched,
+    wcopy, wide, mixed, stock, turned, fetched, kept,
 ):
     r, c = lax.axis_index("row"), lax.axis_index("col")
     row = Line("row", rows_n, lambda index: (index, c))
@@ -301,15 +302,18 @@
                     found = look(s, found)
             else:
                 found = lax.fori_loop(0, slots, look, found)
-            piece = stock[found]
             if per == 1:
                 rows, lead = pl.ds(0, block), i
             else:
                 rows, lead = pl.ds((i % per) * block, block), i // per
-            dense[lead, rows, j * block:(j + 1) * block] = piece
-            flipped[lead, j * block:(j + 1) * block, rows] = piece.T
+            dense[lead, rows, j * block:(j + 1) * block] = stock[found]
+            flipped[lead, j * block:(j + 1) * block, rows] = turned[found]
+
+    def turn(s):
+        turned[s] = stock[s].T
 
     fetch_values.wait()
+    each(slots + 1, turn)
     half = row_blocks // 2
     each(half, place)
     each(row.outer - 1, lambda k: xs.relay(0, k))
@@ -321,16 +325,24 @@
 
     tall = own // PARTS
 
-    def forward(p, index):
-        rows = dense[index, p * tall:(p + 1) * tall, :]
-        return jnp.concatenate(
-            [dot(rows, xg[h].reshape(rows_n * own, width)) for h in range(PARTS)], axis=1)
+    def forward(p, side):
+        rows = jnp.concatenate(
+            [dense[o2 * col.inner + side, p * tall:(p + 1) * tall, :] for o2 in range(col.outer)], axis=0)
+        full = jnp.concatenate([xg[h].reshape(rows_n * own, width) for h in range(PARTS)], axis=1)
+        return dot(rows, full).reshape(col.outer, tall, hidden)
+
+    def kept_block(p, index):
+        return kept[p, index // col.inner]
 
     for h in range(PARTS):
         if row.inner == 2:
             each(row.outer, lambda k: xs.passed(h, k))
     for p in range(PARTS):
-        agg.start(p, forward)
+        if col.inner == 2:
+            c_near[p] = forward(p, 1 - col.i).astype(BF16)
+        agg.start(p, None)
+    for p in range(PARTS):
+        kept[p] = forward(p, col.i)
     fetch_weight.wait()
     wcopy[...] = wide[...].astype(BF16)
 
@@ -350,10 +362,10 @@
     hops = col.outer - 1
     for p in range(PARTS):
         early = (hops + 1) // 2 if p else hops
-        agg.middle(p, forward, 0, early)
+        agg.middle(p, kept_block, 0, early)
         if p:
             own_slope(p - 1)
-            agg.middle(p, forward, early, hops)
+            agg.middle(p, kept_block, early, hops)
             each(min(hops, 1), lambda k: slopes.relay(k, p - 1, None))
     own_slope(PARTS - 1)
 
@@ -369,19 +381,25 @@
 
     each(rows_n - 1, lambda k: w1_copy(k).start())
 
-    def backward(h, index):
-        return dot(flipped[index], both(index)[:, h * width:(h + 1) * width])
-
-    def add(index):
+    def add(index, h):
+        pair = [(index // col.inner) * col.inner + i for i in range(col.inner)]
+        span = slice(h * width, (h + 1) * width)
+        left = jnp.concatenate([flipped[i] for i in pair], axis=1)
+        right = jnp.concatenate([sg[p, i, :, span] for i in pair for p in range(PARTS)], axis=0)
+        grad[h] += dot(left, right)
+
+    def add_all(index):
         for h in range(PARTS):
-            grad[h] += backward(h, index)
-
+            add(index, h)
+
+    for h in range(PARTS):
+        grad[h] = jnp.zeros(grad.shape[1:], F32)
+    alone = add_all if col.inner == 1 else None
     for p in range(PARTS):
         seen = min(hops, 1) if p < PARTS - 1 else 0
-        each(hops - seen, lambda k: slopes.relay(seen + k, p, add if p == PARTS - 1 else None))
-        if p == 0:
-            for h in range(PARTS):
-                grad[h] = backward(h, c)
+        each(hops - seen, lambda k: slopes.relay(seen + k, p, alone if p == PARTS - 1 else None))
+    if col.inner == 1:
+        add_all(c)
 
     nodes = Scatter(row, e_near, e_near_in, e_far, e_far_in, e_total, (e_ns, e_nl, e_fs, e_fl))
 
@@ -412,7 +430,7 @@
 
     for p in range(PARTS):
         if col.inner == 2:
-            use = add if p == PARTS - 1 else None
+            use = add_all if p == PARTS - 1 else None
             slopes.passed(-1, p, use)
             each(hops, lambda k: slopes.passed(k, p, use))
     for h in range(PARTS):
@@ -499,7 +517,9 @@
             pltpu.VMEM((hidden, hidden), F32),
             pltpu.VMEM((own, hidden), BF16),
             pltpu.VMEM((values.shape[0] + 1,) + values.shape[1:], BF16),
+            pltpu.VMEM((values.shape[0] + 1,) + values.shape[1:], BF16),
             dma((2,)),
+            pltpu.VMEM((PARTS, col_out, own // PARTS, hidden), F32),
         ]
     )
     vmem = pl.BlockSpec(memory_space=pltpu.VMEM)
@@ -518,7 +538,7 @@
             collective_id=0, has_side_effects=True, vmem_limit_bytes=56 * 1024 * 1024
         ),
     )(coords, features, weight, cotangent, values)
-    ours, theirs, turned = pl.pallas_call(
+    ours, theirs, flat = pl.pallas_call(
         hand_over,
         out_shape=tuple(jax.ShapeDtypeStruct(a.shape, a.dtype) for a in results),
         in_specs=[pl.BlockSpec(memory_space=pltpu.HBM)] * 3,
@@ -526,7 +546,7 @@
         scratch_shapes=[pltpu.VMEM(a.shape, a.dtype) for a in results] + [dma((2, 3))],
         compiler_params=pltpu.CompilerParams(vmem_limit_bytes=60 * 1024 * 1024),
     )(*results)
-    return ours, theirs, turned.T
+    return ours, theirs, flat.T
 
 
 def solution(mesh):

time: 55.4 us -> 55.3 us (level)
  no operation moved by 1% of the time
where the time goes in v6:
time: 55.3 us; the launch traced here: 55.2 us
  Pallas kernels  54.5 us (99%)
  between operations  0.64 us (1%)
    pallas_call x1, Pallas kernels, on_device(): pl.pallas_call(functools.partial(kernel, rows_n, cols_n, scale), out_shap...  52.7 us
    pallas_call x1, Pallas kernels, on_device(): pl.pallas_call(hand_over, out_shape=tuple((jax.ShapeDtypeStruct(a.shape,...  1.79 us

profile of v6, /device:TPU:0, one launch (start us, length us, event | category | flops | bytes accessed | tf_op | source)
XLA Modules:
  0.0 55.2 jit_solution(7200257804973777821)
XLA Ops:
  0.6 52.7 %shard_map.76 = (f32[128,512]{1,0:T(8,128)}, f32[128,512]{1,0:T(8,128)}, f32[64,128]{1,0:T(8,128)}) custom-call(s32[2,12]{1,0:T(2,128)} %bitcast.4, f32[128,512]{1,0:T(8,128)} %features.1, f32[512,512]{1,0:T(8,128)} %weight.1, bf16[128,512]{1,0:T(8,128)(2,1)} %cotangent.1, bf16[12,128,128]{2,1,0:T(8,128)(2,1)} %bitcast.3), custom_call_target="tpu_custom_call" | custom-call | tf_op jit(solution)/shard_map/pallas_call | solution.py:527
  53.4 1.8 %shard_map.77 = (f32[128,512]{1,0:T(8,128)}, f32[128,512]{1,0:T(8,128)}, f32[64,128]{1,0:T(8,128)}) custom-call(f32[128,512]{1,0:T(8,128)} %get-tuple-element.9.a, f32[128,512]{1,0:T(8,128)} %get-tuple-element.10.b, f32[64,128]{1,0:T(8,128)} %get-tuple-element.11.c), custom_call_target="tpu_custom_call" | custom-call | tf_op jit(solution)/shard_map/pallas_call | solution.py:541

commit v7 on v6

--- a/solution.py
+++ b/solution.py
@@ -248,8 +248,9 @@
 
 def kernel(
     rows_n, cols_n, scale,
-    coords, features, weight, cotangent, values,
-    activated, dfeatures, dweight,
+    coords, features_in, weight, cotangent_in, values,
+    activated_out, dfeatures_out, dweight_out,
+    features, cotangent, activated, dfeatures, dweight, moved,
     xg, xg_sent, xg_landed,
     dense, flipped,
     c_near, c_near_in, c_far, c_far_in, c_total, c_ns, c_nl, c_fs, c_fl,
@@ -274,8 +275,13 @@
         barrier, inc=1, device_id=col.device(lax.rem(c + k + 1, cols_n)), device_id_type=MESH))
     fetch_values = pltpu.make_async_copy(values, stock.at[pl.ds(0, slots)], fetched.at[0])
     fetch_weight = pltpu.make_async_copy(weight, wide, fetched.at[1])
+    fetch_features = pltpu.make_async_copy(features_in, features, moved.at[0])
+    fetch_cotangent = pltpu.make_async_copy(cotangent_in, cotangent, moved.at[1])
+    fetch_features.start()
     fetch_values.start()
+    fetch_cotangent.start()
     fetch_weight.start()
+    fetch_features.wait()
     for h in range(PARTS):
         xg[h, r] = features[:, h * width:(h + 1) * width].astype(BF16)
     stock[slots] = jnp.zeros((block, block), BF16)
@@ -344,6 +350,7 @@
     for p in range(PARTS):
         kept[p] = forward(p, col.i)
     fetch_weight.wait()
+    fetch_cotangent.wait()
     wcopy[...] = wide[...].astype(BF16)
 
     slopes = Chain(col, sg, sg_sent, sg_landed)
@@ -368,6 +375,10 @@
             agg.middle(p, kept_block, early, hops)
             each(min(hops, 1), lambda k: slopes.relay(k, p - 1, None))
     own_slope(PARTS - 1)
+    give_activated = pltpu.make_async_copy(activated, activated_out, moved.at[2])
+    give_dfeatures = pltpu.make_async_copy(dfeatures, dfeatures_out, moved.at[3])
+    give_dweight = pltpu.make_async_copy(dweight, dweight_out, moved.at[4])
+    give_activated.start()
 
     def both(index):
         return jnp.concatenate([sg[p, index] for p in range(PARTS)], axis=0)
@@ -388,18 +399,17 @@
         right = jnp.concatenate([sg[p, i, :, span] for i in pair for p in range(PARTS)], axis=0)
         grad[h] += dot(left, right)
 
-    def add_all(index):
-        for h in range(PARTS):
-            add(index, h)
+    def add_first(index):
+        add(index, 0)
 
     for h in range(PARTS):
         grad[h] = jnp.zeros(grad.shape[1:], F32)
-    alone = add_all if col.inner == 1 else None
+    alone = add_first if col.inner == 1 else None
     for p in range(PARTS):
         seen = min(hops, 1) if p < PARTS - 1 else 0
         each(hops - seen, lambda k: slopes.relay(seen + k, p, alone if p == PARTS - 1 else None))
     if col.inner == 1:
-        add_all(c)
+        add_first(c)
 
     nodes = Scatter(row, e_near, e_near_in, e_far, e_far_in, e_total, (e_ns, e_nl, e_fs, e_fl))
 
@@ -430,13 +440,19 @@
 
     for p in range(PARTS):
         if col.inner == 2:
-            use = add_all if p == PARTS - 1 else None
+            use = add_first if p == PARTS - 1 else None
             slopes.passed(-1, p, use)
             each(hops, lambda k: slopes.passed(k, p, use))
     for h in range(PARTS):
+        if h:
+            each(col.outer, lambda k: add(k * col.inner, h))
         nodes.start(h, term)
     for h in range(PARTS):
         nodes.middle(h, term, 0, row.outer - 1)
+
+    each(cols_n - 1, w2_wait)
+    dweight[...] = jnp.sum(w2_in[...].astype(F32), axis=0) * scale
+    give_dweight.start()
 
     out = None
     for h in range(PARTS):
@@ -444,9 +460,7 @@
         piece = dot(grad16, wcopy[:, h * width:(h + 1) * width], 1, 1)
         out = piece if out is None else out + piece
     dfeatures[...] = out
-
-    each(cols_n - 1, w2_wait)
-    dweight[...] = jnp.sum(w2_in[...].astype(F32), axis=0) * scale
+    give_dfeatures.start()
 
     for h in range(PARTS):
         xs.drain(h)
@@ -455,6 +469,8 @@
         nodes.drain(h)
     each(rows_n - 1, lambda k: w1_copy(k).wait_send())
     each(cols_n - 1, lambda k: w2_copy(k).wait_send())
+    for give in (give_activated, give_dweight, give_dfeatures):
+        give.wait()
 
 
 def hand_over(a, b, c, a_out, b_out, c_out, a_held, b_held, c_held, sems):
@@ -495,7 +511,15 @@
         )
 
     scratch = (
-        gather_scratch(rows_n, row_out)
+        [
+            pltpu.VMEM((own, hidden), F32),
+            pltpu.VMEM((own, hidden), BF16),
+            pltpu.VMEM((own, hidden), F32),
+            pltpu.VMEM((own, hidden), F32),
+            pltpu.VMEM((share_c, share_r), F32),
+            dma((5,)),
+        ]
+        + gather_scratch(rows_n, row_out)
         + [
             pltpu.VMEM((cols_n, own, rows_n * own), BF16),
             pltpu.VMEM((cols_n, rows_n * own, own), BF16),
@@ -522,7 +546,6 @@
             pltpu.VMEM((PARTS, col_out, own // PARTS, hidden), F32),
         ]
     )
-    vmem = pl.BlockSpec(memory_space=pltpu.VMEM)
     anywhere = pl.BlockSpec(memory_space=pl.ANY)
     results = pl.pallas_call(
         functools.partial(kernel, rows_n, cols_n, scale),
@@ -531,8 +554,8 @@
             jax.ShapeDtypeStruct((own, hidden), F32),
             jax.ShapeDtypeStruct((share_c, share_r), F32),
         ),
-        in_specs=[pl.BlockSpec(memory_space=pltpu.SMEM), vmem, anywhere, vmem, anywhere],
-        out_specs=(vmem, vmem, vmem),
+        in_specs=[pl.BlockSpec(memory_space=pltpu.SMEM)] + [anywhere] * 4,
+        out_specs=(anywhere,) * 3,
         scratch_shapes=scratch,
         compiler_params=pltpu.CompilerParams(
             collective_id=0, has_side_effects=True, vmem_limit_bytes=56 * 1024 * 1024

time: 55.3 us -> 55.9 us (1.011)
  Pallas kernels: 54.5 us -> 55.1 us
    pallas_call x1, Pallas kernels: 52.7 us -> 53.3 us  [on_device(): pl.pallas_call(functools.partial(kernel, rows_n, cols_n, scale), out_shap...]
where the time goes in v7:
time: 55.9 us; the launch traced here: 55.8 us
  Pallas kernels  55.1 us (99%)
  between operations  0.64 us (1%)
    pallas_call x1, Pallas kernels, on_device(): pl.pallas_call(functools.partial(kernel, rows_n, cols_n, scale), out_shap...  53.3 us
    pallas_call x1, Pallas kernels, on_device(): pl.pallas_call(hand_over, out_shape=tuple((jax.ShapeDtypeStruct(a.shape,...  1.79 us

profile of v7, /device:TPU:0, one launch (start us, length us, event | category | flops | bytes accessed | tf_op | source)
XLA Modules:
  0.0 55.8 jit_solution(10288407283037192384)
XLA Ops:
  0.6 53.3 %shard_map.76 = (f32[128,512]{1,0:T(8,128)}, f32[128,512]{1,0:T(8,128)}, f32[64,128]{1,0:T(8,128)}) custom-call(s32[2,12]{1,0:T(2,128)} %bitcast.4, f32[128,512]{1,0:T(8,128)} %features_in.1, f32[512,512]{1,0:T(8,128)} %weight.1, bf16[128,512]{1,0:T(8,128)(2,1)} %cotangent_in.1, bf16[12,128,128]{2,1,0:T(8,128)(2,1)} %bitcast.3), custom_call_target="tpu_custom_call" | custom-call | tf_op jit(solution)/shard_map/pallas_call | solution.py:550
  54.0 1.8 %shard_map.77 = (f32[128,512]{1,0:T(8,128)}, f32[128,512]{1,0:T(8,128)}, f32[64,128]{1,0:T(8,128)}) custom-call(f32[128,512]{1,0:T(8,128)} %get-tuple-element.9.a, f32[128,512]{1,0:T(8,128)} %get-tuple-element.10.b, f32[64,128]{1,0:T(8,128)} %get-tuple-element.11.c), custom_call_target="tpu_custom_call" | custom-call | tf_op jit(solution)/shard_map/pallas_call | solution.py:564

commit v8 on v7

--- a/solution.py
+++ b/solution.py
@@ -179,16 +179,21 @@
 
 
 class Scatter:
-    def __init__(self, line, near, near_in, far, far_in, total, sems):
+    def __init__(self, line, near, near_in, far, far_in, total, sems, cuts):
+        self.cuts = cuts
         self.line, self.total = line, total
         self.near, self.near_in, self.far, self.far_in = near, near_in, far, far_in
         self.near_sent, self.near_landed, self.far_sent, self.far_landed = sems
 
-    def near_copy(self, h, o2):
-        return remote(
-            self.near.at[h, o2], self.near_in.at[h, o2], self.near_sent.at[h, o2],
-            self.near_landed.at[h, o2], self.line.mate(),
-        )
+    def near_copies(self, h, o2):
+        cuts = self.cuts[h]
+        width = self.near.shape[-1] // cuts
+        for cut in range(cuts):
+            span = pl.ds(cut * width, width)
+            yield remote(
+                self.near.at[h, o2, :, span], self.near_in.at[h, o2, :, span],
+                self.near_sent.at[cut, h, o2], self.near_landed.at[cut, h, o2], self.line.mate(),
+            )
 
     def far_copy(self, h, o2, source):
         return remote(
@@ -196,14 +201,16 @@
             self.far_landed.at[h, source], self.line.device(o2 * self.line.inner + self.line.i),
         )
 
-    def start(self, h, partial):
+    def start(self, h, partial, cut=None):
         line = self.line
 
         def one(k):
             o2 = line.ahead(k)
             if partial is not None:
                 self.near[h, o2] = partial(h, o2 * line.inner + 1 - line.i).astype(BF16)
-            self.near_copy(h, o2).start()
+            for number, copy in enumerate(self.near_copies(h, o2)):
+                if cut is None or cut == number:
+                    copy.start()
 
         if line.inner == 2:
             each(line.outer, one)
@@ -212,7 +219,8 @@
         line = self.line
         value = partial(h, o2 * line.inner + line.i)
         if line.inner == 2:
-            self.near_copy(h, o2).wait_recv()
+            for copy in self.near_copies(h, o2):
+                copy.wait_recv()
             value = value + self.near_in[h, o2].astype(F32)
         return value
 
@@ -242,7 +250,7 @@
     def drain(self, h):
         line = self.line
         if line.inner == 2:
-            each(line.outer, lambda k: self.near_copy(h, k).wait_send())
+            each(line.outer, lambda k: [copy.wait_send() for copy in self.near_copies(h, k)])
         each(line.outer - 1, lambda k: self.far_copy(h, line.ahead(k), line.o).wait_send())
 
 
@@ -327,15 +335,16 @@
     for h in range(1, PARTS):
         each(row.outer - 1, lambda k: xs.relay(h, k))
 
-    agg = Scatter(col, c_near, c_near_in, c_far, c_far_in, c_total, (c_ns, c_nl, c_fs, c_fl))
+    agg = Scatter(col, c_near, c_near_in, c_far, c_far_in, c_total, (c_ns, c_nl, c_fs, c_fl),
+                  (PARTS,) + (1,) * (PARTS - 1))
 
     tall = own // PARTS
 
-    def forward(p, side):
+    def forward(p, side, parts):
         rows = jnp.concatenate(
             [dense[o2 * col.inner + side, p * tall:(p + 1) * tall, :] for o2 in range(col.outer)], axis=0)
-        full = jnp.concatenate([xg[h].reshape(rows_n * own, width) for h in range(PARTS)], axis=1)
-        return dot(rows, full).reshape(col.outer, tall, hidden)
+        full = jnp.concatenate([xg[h].reshape(rows_n * own, width) for h in parts], axis=1)
+        return dot(rows, full).reshape(col.outer, tall, full.shape[1])
 
     def kept_block(p, index):
         return kept[p, index // col.inner]
@@ -343,12 +352,15 @@
     for h in range(PARTS):
         if row.inner == 2:
             each(row.outer, lambda k: xs.passed(h, k))
+        if col.inner == 2:
+            c_near[0, :, :, h * width:(h + 1) * width] = forward(0, 1 - col.i, (h,)).astype(BF16)
+            agg.start(0, None, h)
+    for p in range(1, PARTS):
+        if col.inner == 2:
+            c_near[p] = forward(p, 1 - col.i, range(PARTS)).astype(BF16)
+            agg.start(p, None)
     for p in range(PARTS):
-        if col.inner == 2:
-            c_near[p] = forward(p, 1 - col.i).astype(BF16)
-        agg.start(p, None)
-    for p in range(PARTS):
-        kept[p] = forward(p, col.i)
+        kept[p] = forward(p, col.i, range(PARTS))
     fetch_weight.wait()
     fetch_cotangent.wait()
     wcopy[...] = wide[...].astype(BF16)
@@ -411,7 +423,8 @@
     if col.inner == 1:
         add_first(c)
 
-    nodes = Scatter(row, e_near, e_near_in, e_far, e_far_in, e_total, (e_ns, e_nl, e_fs, e_fl))
+    nodes = Scatter(row, e_near, e_near_in, e_far, e_far_in, e_total, (e_ns, e_nl, e_fs, e_fl),
+                    (1,) * PARTS)
 
     def term(h, index):
         return grad[h, pl.ds(pl.multiple_of(index * own, own), own), :]
@@ -507,7 +520,8 @@
         return (
             [pltpu.VMEM((PARTS, outer) + piece, BF16)] * 4
             + [pltpu.VMEM((PARTS,) + piece, F32)]
-            + [dma((PARTS, outer))] * 4
+            + [dma((PARTS, PARTS, outer))] * 2
+            + [dma((PARTS, outer))] * 2
         )
 
     scratch = (

time: 55.9 us -> 56.7 us (1.014)
  Pallas kernels: 55.1 us -> 55.9 us
    pallas_call x1, Pallas kernels: 53.3 us -> 54.1 us  [on_device(): pl.pallas_call(functools.partial(kernel, rows_n, cols_n, scale), out_shap...]
where the time goes in v8:
time: 56.7 us; the launch traced here: 56.6 us
  Pallas kernels  55.9 us (99%)
  between operations  0.64 us (1%)
    pallas_call x1, Pallas kernels, on_device(): pl.pallas_call(functools.partial(kernel, rows_n, cols_n, scale), out_shap...  54.1 us
    pallas_call x1, Pallas kernels, on_device(): pl.pallas_call(hand_over, out_shape=tuple((jax.ShapeDtypeStruct(a.shape,...  1.79 us

profile of v8, /device:TPU:0, one launch (start us, length us, event | category | flops | bytes accessed | tf_op | source)
XLA Modules:
  0.0 56.6 jit_solution(7328007470639690424)
XLA Ops:
  0.6 54.1 %shard_map.76 = (f32[128,512]{1,0:T(8,128)}, f32[128,512]{1,0:T(8,128)}, f32[64,128]{1,0:T(8,128)}) custom-call(s32[2,12]{1,0:T(2,128)} %bitcast.4, f32[128,512]{1,0:T(8,128)} %features_in.1, f32[512,512]{1,0:T(8,128)} %weight.1, bf16[128,512]{1,0:T(8,128)(2,1)} %cotangent_in.1, bf16[12,128,128]{2,1,0:T(8,128)(2,1)} %bitcast.3), custom_call_target="tpu_custom_call" | custom-call | tf_op jit(solution)/shard_map/pallas_call | solution.py:564
  54.8 1.8 %shard_map.77 = (f32[128,512]{1,0:T(8,128)}, f32[128,512]{1,0:T(8,128)}, f32[64,128]{1,0:T(8,128)}) custom-call(f32[128,512]{1,0:T(8,128)} %get-tuple-element.9.a, f32[128,512]{1,0:T(8,128)} %get-tuple-element.10.b, f32[64,128]{1,0:T(8,128)} %get-tuple-element.11.c), custom_call_target="tpu_custom_call" | custom-call | tf_op jit(solution)/shard_map/pallas_call | solution.py:578

commit v9 on v6

--- a/solution.py
+++ b/solution.py
@@ -49,6 +49,20 @@
     def behind(self, k):
         return lax.rem(self.o + self.outer - k - 1, self.outer)
 
+    def offset(self, k):
+        if self.outer == 1:
+            return 0
+        hops = (k + self.outer // 2 - 1) % (self.outer - 1) + 1
+        if isinstance(k, int):
+            return hops if k < self.outer - 1 else 0
+        return jnp.where(k < self.outer - 1, hops, 0)
+
+    def ahead_far(self, k):
+        return lax.rem(self.o + self.offset(k), self.outer)
+
+    def behind_far(self, k):
+        return lax.rem(self.o + self.outer - self.offset(k), self.outer)
+
     def mate(self):
         return self.device(self.o * self.inner + 1 - self.i)
 
@@ -200,7 +214,7 @@
         line = self.line
 
         def one(k):
-            o2 = line.ahead(k)
+            o2 = line.ahead_far(k)
             if partial is not None:
                 self.near[h, o2] = partial(h, o2 * line.inner + 1 - line.i).astype(BF16)
             self.near_copy(h, o2).start()
@@ -220,7 +234,7 @@
         line = self.line
 
         def one(k):
-            o2 = line.ahead(first + k)
+            o2 = line.ahead_far(first + k)
             self.far[h, o2] = self.pair(h, o2, partial).astype(BF16)
             self.far_copy(h, o2, line.o).start()
 
@@ -232,8 +246,8 @@
         line = self.line
 
         def one(k):
-            source = line.behind(k)
-            self.far_copy(h, line.ahead(0), source).wait_recv()
+            source = line.behind_far(k)
+            self.far_copy(h, line.ahead_far(0), source).wait_recv()
             self.total[h] += self.far_in[h, source].astype(F32)
 
         each(line.outer - 1, one)
@@ -243,7 +257,7 @@
         line = self.line
         if line.inner == 2:
             each(line.outer, lambda k: self.near_copy(h, k).wait_send())
-        each(line.outer - 1, lambda k: self.far_copy(h, line.ahead(k), line.o).wait_send())
+        each(line.outer - 1, lambda k: self.far_copy(h, line.ahead_far(k), line.o).wait_send())
 
 
 def kernel(

time: 55.3 us -> 53.9 us (0.975)
  Pallas kernels: 54.5 us -> 53.1 us
    pallas_call x1, Pallas kernels: 52.7 us -> 51.3 us  [on_device(): pl.pallas_call(functools.partial(kernel, rows_n, cols_n, scale), out_shap...]
where the time goes in v9:
time: 53.9 us; the launch traced here: 53.7 us
  Pallas kernels  53.1 us (99%)
  between operations  0.64 us (1%)
    pallas_call x1, Pallas kernels, on_device(): pl.pallas_call(functools.partial(kernel, rows_n, cols_n, scale), out_shap...  51.3 us
    pallas_call x1, Pallas kernels, on_device(): pl.pallas_call(hand_over, out_shape=tuple((jax.ShapeDtypeStruct(a.shape,...  1.79 us

profile of v9, /device:TPU:0, one launch (start us, length us, event | category | flops | bytes accessed | tf_op | source)
XLA Modules:
  0.0 53.7 jit_solution(5984820262706245942)
XLA Ops:
  0.6 51.3 %shard_map.76 = (f32[128,512]{1,0:T(8,128)}, f32[128,512]{1,0:T(8,128)}, f32[64,128]{1,0:T(8,128)}) custom-call(s32[2,12]{1,0:T(2,128)} %bitcast.4, f32[128,512]{1,0:T(8,128)} %features.1, f32[512,512]{1,0:T(8,128)} %weight.1, bf16[128,512]{1,0:T(8,128)(2,1)} %cotangent.1, bf16[12,128,128]{2,1,0:T(8,128)(2,1)} %bitcast.3), custom_call_target="tpu_custom_call" | custom-call | tf_op jit(solution)/shard_map/pallas_call | solution.py:541
  51.9 1.8 %shard_map.77 = (f32[128,512]{1,0:T(8,128)}, f32[128,512]{1,0:T(8,128)}, f32[64,128]{1,0:T(8,128)}) custom-call(f32[128,512]{1,0:T(8,128)} %get-tuple-element.9.a, f32[128,512]{1,0:T(8,128)} %get-tuple-element.10.b, f32[64,128]{1,0:T(8,128)} %get-tuple-element.11.c), custom_call_target="tpu_custom_call" | custom-call | tf_op jit(solution)/shard_map/pallas_call | solution.py:555
